TPU v7x, 32 devices: a whole 2x2x4 slice. The times are simulated.
32 devices in a mesh: gx: 16 (over z, y, core), gy: 2 (over x).
Axes of the slice: x: 2, y: 2, z: 4, core: 2. Of those that a mesh axis runs over, the one named last changes fastest.
Arguments:
- source: float32 [64, 128, 256], P('gx', 'gy'), may hold values from -5 to 5
- obstacle: int32 [64, 128, 256], P('gx', 'gy'), may hold values from 0 to 1, as said below
Outputs:
- pressure: float32 [64, 128, 256], P('gx', 'gy')
Inputs may be any that keep to these rules, and one draw needn't show every extreme that they name: `obstacle`: 1 marks a cell inside a building, 0 a cell of air.
All inputs are finite; a program needn't handle non-finite values.
Results may differ from a plain program's by a relative error of at most 0.00002.
Values sent between devices are 32-bit elements; how exact they have to be, the bound alone decides.
A program may use at most 64 MiB of HBM per device.

v0:
```python
import jax
import jax.numpy as jnp
from jax import lax
from jax.sharding import PartitionSpec as P

LEVELS = 5


OMEGA = 0.8
PENALTY = 24.0


def padded_2(cells, sides, width):
    for axis, dim in sides:
        count = lax.axis_size(axis)
        ends = count - 1
        head = lax.slice_in_dim(cells, 0, width, axis=dim)
        tail = lax.slice_in_dim(cells, cells.shape[dim] - width, cells.shape[dim], axis=dim)
        cells = jnp.concatenate(
            [
                lax.ppermute(tail, axis, [(i, (i + 1) % count) for i in range(ends)]),
                cells,
                lax.ppermute(head, axis, [((i + 1) % count, i) for i in range(ends)]),
            ],
            axis=dim,
        )
    return cells


def shifted(shard, axis, by):
    count = lax.axis_size(axis)
    pairs = [(i, i + by) for i in range(count) if 0 <= i + by < count]
    return lax.ppermute(shard, axis, pairs)


def partner_2(value, axis, stride):
    mask = 2**stride
    pairs = [(source, source ^ mask) for source in range(lax.axis_size(axis))]
    return lax.ppermute(value, axis, pairs)


def neighbor_sum(padded):
    bordered = jnp.pad(padded, ((0, 0), (0, 0), (1, 1)))
    summed = bordered[2:, 1:-1, 1:-1] + bordered[:-2, 1:-1, 1:-1]
    summed = summed + bordered[1:-1, 2:, 1:-1] + bordered[1:-1, :-2, 1:-1]
    summed = summed + bordered[1:-1, 1:-1, 2:] + bordered[1:-1, 1:-1, :-2]
    return summed


def restrict(residual):
    size_x, size_y, size_z = residual.shape
    blocks = residual.reshape(size_x // 2, 2, size_y // 2, 2, size_z // 2, 2)
    return blocks.sum(axis=(1, 3, 5)) * 0.125


def prolong(correction):
    return jnp.repeat(jnp.repeat(jnp.repeat(correction, 2, 0), 2, 1), 2, 2)


def body(source, obstacle):
    solid_cells = obstacle.astype(jnp.float32)
    source_fluid = (1.0 - solid_cells) * source
    diagonal = 6.0 + PENALTY * solid_cells
    weight = OMEGA / diagonal
    position = lax.axis_index("gx")

    def spread_pad(field):
        return padded_2(field, (("gx", 0), ("gy", 1)), 1)

    def spread_apply(field, grid_level):
        return (6.0 * field - neighbor_sum(spread_pad(field))) * 0.25**grid_level

    def group_apply(field, grid_level):
        from_below = shifted(field[-1:], "gx", 16)
        from_above = shifted(field[:1], "gx", -16)
        stacked = jnp.concatenate([from_below, field, from_above], 0)
        padded = padded_2(stacked, (("gy", 1),), 1)
        return (6.0 * field - neighbor_sum(padded)) * 0.25**grid_level

    def group_cycle(residual, grid_level):
        damping = OMEGA / (6.0 * 0.25**grid_level)
        correction = damping * residual
        if grid_level == LEVELS - 1:
            return correction + damping * (residual - group_apply(correction, grid_level))
        leftover = residual - group_apply(correction, grid_level)
        correction = correction + prolong(group_cycle(restrict(leftover), grid_level + 1))
        return correction + damping * (residual - group_apply(correction, grid_level))

    damping_one = OMEGA / (6.0 * 0.25**1)
    damping_two = OMEGA / (6.0 * 0.25**2)
    fine_corr = weight * source_fluid
    fine_padded = spread_pad(fine_corr)
    fine_left = source_fluid - (diagonal * fine_corr - neighbor_sum(fine_padded))
    residual_one = restrict(fine_left)
    corr_one = damping_one * residual_one
    left_one = residual_one - spread_apply(corr_one, 1)
    residual_two = restrict(left_one)
    corr_two = damping_two * residual_two
    left_two = residual_two - spread_apply(corr_two, 2)
    merged = left_two
    bit_order = (0, 1, 2, 3)
    for bit_index in bit_order:
        partner = partner_2(merged, "gx", bit_index)
        upper_half = position >> bit_index & 1 == 1
        merged = jnp.where(
            upper_half, jnp.concatenate([partner, merged], 0), jnp.concatenate([merged, partner], 0)
        )
    group_corr = prolong(group_cycle(restrict(merged), 3))
    own_plane = lax.dynamic_slice_in_dim(group_corr, position % 16, 1, 0)
    corr_two = corr_two + own_plane
    corr_two = corr_two + damping_two * (residual_two - spread_apply(corr_two, 2))
    corr_one = corr_one + prolong(corr_two)
    corr_one = corr_one + damping_one * (residual_one - spread_apply(corr_one, 1))
    fine_corr = fine_corr + prolong(corr_one)
    outer = spread_pad(fine_corr)
    pressure = fine_corr + weight * (source_fluid - (diagonal * fine_corr - neighbor_sum(outer)))
    return pressure


def solution(mesh):
    in_specs = (P("gx", "gy", None), P("gx", "gy", None))
    out_specs = P("gx", "gy", None)
    return jax.shard_map(body, mesh=mesh, in_specs=in_specs, out_specs=out_specs, check_vma=False)
```

profile of v0, /device:TPU:26, one launch (start us, length us, event | category | flops | bytes accessed | tf_op | source)
XLA Modules:
  0.0 187.5 jit_solution(17169265017468433274)
XLA Ops:
  2.5 2.8 %collective-permute-start = (f32[1,64,256]{1,2,0:T(8,128)S(1)}, f32[1,64,256]{1,2,0:T(8,128)S(1)}, u32[]{:S(2)}, u32[]{:S(2)}) collective-permute-start(f32[1,64,256]{1,2,0:T(8,128)S(1)} %get-tuple-element.12), channel_id=1, source_target_pairs={{2,0},{4,2},{6,4},{8,6},{10,8},{12,10},{14,12},{16,14},{18,16},{20... | collective-permute-start | bytes 196616 | tf_op jit(solution)/shard_map/ppermute | solution.py:23
  7.7 4.7 %collective-permute-done.1 = f32[1,64,256]{1,2,0:T(8,128)S(1)} collective-permute-done((f32[1,64,256]{1,2,0:T(8,128)S(1)}, f32[1,64,256]{1,2,0:T(8,128)S(1)}, u32[]{:S(2)}, u32[]{:S(2)}) %collective-permute-start.1) | collective-permute-done | bytes 65568 | tf_op jit(solution)/shard_map/ppermute | solution.py:21
  13.0 2.4 %collective-permute-start.2 = (f32[6,1,256]{2,1,0:T(1,128)S(1)}, f32[6,1,256]{2,1,0:T(1,128)S(1)}, u32[]{:S(2)}, u32[]{:S(2)}) collective-permute-start(f32[6,1,256]{2,1,0:T(1,128)S(1)} %copy.79), channel_id=1, source_target_pairs={{1,0},{3,2},{5,4},{7,6},{9,8},{11,10},{13,12},{15,14},{17,16},{19,... | collective-permute-start | bytes 18440 | tf_op jit(solution)/shard_map/ppermute | solution.py:23
  17.4 3.9 %collective-permute-done.3 = f32[6,1,256]{2,1,0:T(1,128)S(1)} collective-permute-done((f32[6,1,256]{2,1,0:T(1,128)S(1)}, f32[6,1,256]{2,1,0:T(1,128)S(1)}, u32[]{:S(2)}, u32[]{:S(2)}) %collective-permute-start.3) | collective-permute-done | bytes 6176 | tf_op jit(solution)/shard_map/ppermute | solution.py:21
  24.9 18.1 %reshape.76 = f32[2,2,32,2,128,2]{5,4,3,2,1,0:T(8,128)} reshape(f32[4,64,256]{2,1,0:T(8,128)S(1)} %copy.85) | data formatting | bytes 524288 | tf_op jit(solution)/shard_map/reshape | solution.py:52
  42.9 7.0 %reduce_sum.43 = f32[2,32,128]{2,1,0:T(8,128)S(1)} reduce(f32[2,2,32,2,128,2]{5,4,3,2,1,0:T(8,128)} %reshape.76, f32[]{:T(128)} %constant.22.clone.1), dimensions={1,3,5}, to_apply=%region_0.1 | reduce | flops 57344 | bytes 294916 | tf_op jit(solution)/shard_map/reduce_sum | solution.py:53
  54.3 3.5 %collective-permute-done.5 = f32[1,32,128]{2,1,0:T(8,128)S(1)} collective-permute-done((f32[1,32,128]{2,1,0:T(8,128)S(1)}, f32[1,32,128]{2,1,0:T(8,128)S(1)}, u32[]{:S(2)}, u32[]{:S(2)}) %collective-permute-start.5) | collective-permute-done | bytes 16416 | tf_op jit(solution)/shard_map/ppermute | solution.py:21
  60.8 4.2 %collective-permute-done.7 = f32[4,1,128]{2,1,0:T(1,128)S(1)} collective-permute-done((f32[4,1,128]{2,1,0:T(1,128)S(1)}, f32[4,1,128]{2,1,0:T(1,128)S(1)}, u32[]{:S(2)}, u32[]{:S(2)}) %collective-permute-start.7) | collective-permute-done | bytes 2080 | tf_op jit(solution)/shard_map/ppermute | solution.py:21
  70.8 3.4 %collective-permute-done.9 = f32[1,16,64]{2,1,0:T(8,128)S(1)} collective-permute-done((f32[1,16,64]{2,1,0:T(8,128)S(1)}, f32[1,16,64]{2,1,0:T(8,128)S(1)}, u32[]{:S(2)}, u32[]{:S(2)}) %collective-permute-start.9) | collective-permute-done | bytes 4128 | tf_op jit(solution)/shard_map/ppermute | solution.py:21
  77.2 4.2 %collective-permute-done.11 = f32[3,1,64]{2,1,0:T(1,128)S(1)} collective-permute-done((f32[3,1,64]{2,1,0:T(1,128)S(1)}, f32[3,1,64]{2,1,0:T(1,128)S(1)}, u32[]{:S(2)}, u32[]{:S(2)}) %collective-permute-start.11) | collective-permute-done | bytes 800 | tf_op jit(solution)/shard_map/ppermute | solution.py:21
  82.7 3.7 %collective-permute-done.13 = f32[2,16,64]{2,1,0:T(8,128)S(1)} collective-permute-done((f32[2,16,64]{2,1,0:T(8,128)S(1)}, f32[2,16,64]{2,1,0:T(8,128)S(1)}, u32[]{:S(2)}, u32[]{:S(2)}) %collective-permute-start.13) | collective-permute-done | bytes 8224 | tf_op jit(solution)/shard_map/ppermute | solution.py:39
  86.9 3.5 %collective-permute-done.14 = f32[4,16,64]{2,1,0:T(8,128)S(1)} collective-permute-done((f32[4,16,64]{2,1,0:T(8,128)S(1)}, f32[4,16,64]{2,1,0:T(8,128)S(1)}, u32[]{:S(2)}, u32[]{:S(2)}) %collective-permute-start.14) | collective-permute-done | bytes 16416 | tf_op jit(solution)/shard_map/ppermute | solution.py:39
  90.8 5.4 %collective-permute-done.15 = f32[8,16,64]{2,1,0:T(8,128)S(1)} collective-permute-done((f32[8,16,64]{2,1,0:T(8,128)S(1)}, f32[8,16,64]{2,1,0:T(8,128)S(1)}, u32[]{:S(2)}, u32[]{:S(2)}) %collective-permute-start.15) | collective-permute-done | bytes 32800 | tf_op jit(solution)/shard_map/ppermute | solution.py:39
  96.2 5.7 %select_n.54 = f32[8,2,8,2,32,2]{5,4,3,2,1,0:T(8,128)} reshape(f32[16,16,64]{2,1,0:T(8,128)S(1)} %maximum_select_fusion) | data formatting | bytes 131072 | tf_op jit(solution)/shard_map/jit(_where)/select_n | solution.py:105
  101.9 2.6 %reduce_sum.47 = f32[8,8,32]{2,1,0:T(8,128)S(1)} reduce(f32[8,2,8,2,32,2]{5,4,3,2,1,0:T(8,128)} %select_n.54, f32[]{:T(128)} %constant.22.clone.1), dimensions={1,3,5}, to_apply=%region_3.4 | reduce | flops 14336 | bytes 73732 | tf_op jit(solution)/shard_map/reduce_sum | solution.py:53
  108.8 4.2 %collective-permute-done.19 = f32[10,1,32]{2,1,0:T(1,128)S(1)} collective-permute-done((f32[10,1,32]{2,1,0:T(1,128)S(1)}, f32[10,1,32]{2,1,0:T(1,128)S(1)}, u32[]{:S(2)}, u32[]{:S(2)}) %collective-permute-start.19) | collective-permute-done | bytes 1312 | tf_op jit(solution)/shard_map/ppermute | solution.py:21
  118.0 4.2 %collective-permute-done.23 = f32[6,1,16]{2,1,0:T(1,128)S(1)} collective-permute-done((f32[6,1,16]{2,1,0:T(1,128)S(1)}, f32[6,1,16]{2,1,0:T(1,128)S(1)}, u32[]{:S(2)}, u32[]{:S(2)}) %collective-permute-start.23) | collective-permute-done | bytes 416 | tf_op jit(solution)/shard_map/ppermute | solution.py:21
  127.0 4.2 %collective-permute-done.27 = f32[10,1,32]{2,1,0:T(1,128)S(1)} collective-permute-done((f32[10,1,32]{2,1,0:T(1,128)S(1)}, f32[10,1,32]{2,1,0:T(1,128)S(1)}, u32[]{:S(2)}, u32[]{:S(2)}) %collective-permute-start.27) | collective-permute-done | bytes 1312 | tf_op jit(solution)/shard_map/ppermute | solution.py:21
  136.1 3.4 %collective-permute-done.29 = f32[1,16,64]{2,1,0:T(8,128)S(1)} collective-permute-done((f32[1,16,64]{2,1,0:T(8,128)S(1)}, f32[1,16,64]{2,1,0:T(8,128)S(1)}, u32[]{:S(2)}, u32[]{:S(2)}) %collective-permute-start.29) | collective-permute-done | bytes 4128 | tf_op jit(solution)/shard_map/ppermute | solution.py:21
  142.5 4.2 %collective-permute-done.31 = f32[3,1,64]{2,1,0:T(1,128)S(1)} collective-permute-done((f32[3,1,64]{2,1,0:T(1,128)S(1)}, f32[3,1,64]{2,1,0:T(1,128)S(1)}, u32[]{:S(2)}, u32[]{:S(2)}) %collective-permute-start.31) | collective-permute-done | bytes 800 | tf_op jit(solution)/shard_map/ppermute | solution.py:21
  151.5 3.5 %collective-permute-done.33 = f32[1,32,128]{2,1,0:T(8,128)S(1)} collective-permute-done((f32[1,32,128]{2,1,0:T(8,128)S(1)}, f32[1,32,128]{2,1,0:T(8,128)S(1)}, u32[]{:S(2)}, u32[]{:S(2)}) %collective-permute-start.33) | collective-permute-done | bytes 16416 | tf_op jit(solution)/shard_map/ppermute | solution.py:21
  158.0 4.2 %collective-permute-done.35 = f32[4,1,128]{2,1,0:T(1,128)S(1)} collective-permute-done((f32[4,1,128]{2,1,0:T(1,128)S(1)}, f32[4,1,128]{2,1,0:T(1,128)S(1)}, u32[]{:S(2)}, u32[]{:S(2)}) %collective-permute-start.35) | collective-permute-done | bytes 2080 | tf_op jit(solution)/shard_map/ppermute | solution.py:21
  167.3 4.7 %collective-permute-done.37 = f32[1,64,256]{1,2,0:T(8,128)S(1)} collective-permute-done((f32[1,64,256]{1,2,0:T(8,128)S(1)}, f32[1,64,256]{1,2,0:T(8,128)S(1)}, u32[]{:S(2)}, u32[]{:S(2)}) %collective-permute-start.37) | collective-permute-done | bytes 65568 | tf_op jit(solution)/shard_map/ppermute | solution.py:21
  178.1 3.9 %collective-permute-done.39 = f32[6,1,256]{2,1,0:T(1,128)S(1)} collective-permute-done((f32[6,1,256]{2,1,0:T(1,128)S(1)}, f32[6,1,256]{2,1,0:T(1,128)S(1)}, u32[]{:S(2)}, u32[]{:S(2)}) %collective-permute-start.39) | collective-permute-done | bytes 6176 | tf_op jit(solution)/shard_map/ppermute | solution.py:21
  (146 shorter events, 75.1 us)
Async XLA Ops:
  2.5 5.3 %collective-permute-start = (f32[1,64,256]{1,2,0:T(8,128)S(1)}, f32[1,64,256]{1,2,0:T(8,128)S(1)}, u32[]{:S(2)}, u32[]{:S(2)}) collective-permute-start(f32[1,64,256]{1,2,0:T(8,128)S(1)} %get-tuple-element.12), channel_id=1, source_target_pairs={{2,0},{4,2},{6,4},{8,6},{10,8},{12,10},{14,12},{16,14},{18,16},{20... | collective-permute-start | bytes 196616 | tf_op jit(solution)/shard_map/ppermute | solution.py:23
  5.2 7.2 %collective-permute-start.1 = (f32[1,64,256]{1,2,0:T(8,128)S(1)}, f32[1,64,256]{1,2,0:T(8,128)S(1)}, u32[]{:S(2)}, u32[]{:S(2)}) collective-permute-start(f32[1,64,256]{1,2,0:T(8,128)S(1)} %get-tuple-element.11), channel_id=1, source_target_pairs={{0,2},{2,4},{4,6},{6,8},{8,10},{10,12},{12,14},{14,16},{16,18},{18... | collective-permute-start | bytes 196616 | tf_op jit(solution)/shard_map/ppermute | solution.py:21
  13.0 4.0 %collective-permute-start.2 = (f32[6,1,256]{2,1,0:T(1,128)S(1)}, f32[6,1,256]{2,1,0:T(1,128)S(1)}, u32[]{:S(2)}, u32[]{:S(2)}) collective-permute-start(f32[6,1,256]{2,1,0:T(1,128)S(1)} %copy.79), channel_id=1, source_target_pairs={{1,0},{3,2},{5,4},{7,6},{9,8},{11,10},{13,12},{15,14},{17,16},{19,... | collective-permute-start | bytes 18440 | tf_op jit(solution)/shard_map/ppermute | solution.py:23
  15.7 5.5 %collective-permute-start.3 = (f32[6,1,256]{2,1,0:T(1,128)S(1)}, f32[6,1,256]{2,1,0:T(1,128)S(1)}, u32[]{:S(2)}, u32[]{:S(2)}) collective-permute-start(f32[6,1,256]{2,1,0:T(1,128)S(1)} %copy.81), channel_id=1, source_target_pairs={{0,1},{2,3},{4,5},{6,7},{8,9},{10,11},{12,13},{14,15},{16,17},{18,... | collective-permute-start | bytes 18440 | tf_op jit(solution)/shard_map/ppermute | solution.py:21
  49.9 4.3 %collective-permute-start.4 = (f32[1,32,128]{2,1,0:T(8,128)S(1)}, f32[1,32,128]{2,1,0:T(8,128)S(1)}, u32[]{:S(2)}, u32[]{:S(2)}) collective-permute-start(f32[1,32,128]{2,1,0:T(8,128)S(1)} %get-tuple-element.28), channel_id=1, source_target_pairs={{2,0},{4,2},{6,4},{8,6},{10,8},{12,10},{14,12},{16,14},{18,16},{20... | collective-permute-start | bytes 49160 | tf_op jit(solution)/shard_map/ppermute | solution.py:23
  51.9 6.0 %collective-permute-start.5 = (f32[1,32,128]{2,1,0:T(8,128)S(1)}, f32[1,32,128]{2,1,0:T(8,128)S(1)}, u32[]{:S(2)}, u32[]{:S(2)}) collective-permute-start(f32[1,32,128]{2,1,0:T(8,128)S(1)} %get-tuple-element.27), channel_id=1, source_target_pairs={{0,2},{2,4},{4,6},{6,8},{8,10},{10,12},{12,14},{14,16},{16,18},{18... | collective-permute-start | bytes 49160 | tf_op jit(solution)/shard_map/ppermute | solution.py:21
  59.5 5.5 %collective-permute-start.7 = (f32[4,1,128]{2,1,0:T(1,128)S(1)}, f32[4,1,128]{2,1,0:T(1,128)S(1)}, u32[]{:S(2)}, u32[]{:S(2)}) collective-permute-start(f32[4,1,128]{2,1,0:T(1,128)S(1)} %get-tuple-element.15), channel_id=1, source_target_pairs={{0,1},{2,3},{4,5},{6,7},{8,9},{10,11},{12,13},{14,15},{16,17},{18,... | collective-permute-start | bytes 6152 | tf_op jit(solution)/shard_map/ppermute | solution.py:21
  66.4 4.3 %collective-permute-start.8 = (f32[1,16,64]{2,1,0:T(8,128)S(1)}, f32[1,16,64]{2,1,0:T(8,128)S(1)}, u32[]{:S(2)}, u32[]{:S(2)}) collective-permute-start(f32[1,16,64]{2,1,0:T(8,128)S(1)} %multiply_bitcast_fusion), channel_id=1, source_target_pairs={{2,0},{4,2},{6,4},{8,6},{10,8},{12,10},{14,12},{16,14},{18,16},{20... | collective-permute-start | bytes 12296 | tf_op jit(solution)/shard_map/ppermute | solution.py:23
  68.3 5.9 %collective-permute-start.9 = (f32[1,16,64]{2,1,0:T(8,128)S(1)}, f32[1,16,64]{2,1,0:T(8,128)S(1)}, u32[]{:S(2)}, u32[]{:S(2)}) collective-permute-start(f32[1,16,64]{2,1,0:T(8,128)S(1)} %multiply_bitcast_fusion), channel_id=1, source_target_pairs={{0,2},{2,4},{4,6},{6,8},{8,10},{10,12},{12,14},{14,16},{16,18},{18... | collective-permute-start | bytes 12296 | tf_op jit(solution)/shard_map/ppermute | solution.py:21
  75.9 5.5 %collective-permute-start.11 = (f32[3,1,64]{2,1,0:T(1,128)S(1)}, f32[3,1,64]{2,1,0:T(1,128)S(1)}, u32[]{:S(2)}, u32[]{:S(2)}) collective-permute-start(f32[3,1,64]{2,1,0:T(1,128)S(1)} %get-tuple-element.31), channel_id=1, source_target_pairs={{0,1},{2,3},{4,5},{6,7},{8,9},{10,11},{12,13},{14,15},{16,17},{18,... | collective-permute-start | bytes 2312 | tf_op jit(solution)/shard_map/ppermute | solution.py:21
  86.5 3.9 %collective-permute-start.14 = (f32[4,16,64]{2,1,0:T(8,128)S(1)}, f32[4,16,64]{2,1,0:T(8,128)S(1)}, u32[]{:S(2)}, u32[]{:S(2)}) collective-permute-start(f32[4,16,64]{2,1,0:T(8,128)S(1)} %maximum_select_fusion.2), channel_id=1, source_target_pairs={{0,8},{2,10},{4,12},{6,14},{8,0},{10,2},{12,4},{14,6},{16,24},{18,... | collective-permute-start | bytes 49160 | tf_op jit(solution)/shard_map/ppermute | solution.py:39
  90.4 5.8 %collective-permute-start.15 = (f32[8,16,64]{2,1,0:T(8,128)S(1)}, f32[8,16,64]{2,1,0:T(8,128)S(1)}, u32[]{:S(2)}, u32[]{:S(2)}) collective-permute-start(f32[8,16,64]{2,1,0:T(8,128)S(1)} %maximum_select_fusion.1), channel_id=1, source_target_pairs={{0,16},{2,18},{4,20},{6,22},{8,24},{10,26},{12,28},{14,30},{16,0},... | collective-permute-start | bytes 98312 | tf_op jit(solution)/shard_map/ppermute | solution.py:39
  107.5 5.5 %collective-permute-start.19 = (f32[10,1,32]{2,1,0:T(1,128)S(1)}, f32[10,1,32]{2,1,0:T(1,128)S(1)}, u32[]{:S(2)}, u32[]{:S(2)}) collective-permute-start(f32[10,1,32]{2,1,0:T(1,128)S(1)} %get-tuple-element.19), channel_id=1, source_target_pairs={{0,1},{2,3},{4,5},{6,7},{8,9},{10,11},{12,13},{14,15},{16,17},{18,... | collective-permute-start | bytes 3848 | tf_op jit(solution)/shard_map/ppermute | solution.py:21
  116.7 5.5 %collective-permute-start.23 = (f32[6,1,16]{2,1,0:T(1,128)S(1)}, f32[6,1,16]{2,1,0:T(1,128)S(1)}, u32[]{:S(2)}, u32[]{:S(2)}) collective-permute-start(f32[6,1,16]{2,1,0:T(1,128)S(1)} %get-tuple-element.33), channel_id=1, source_target_pairs={{0,1},{2,3},{4,5},{6,7},{8,9},{10,11},{12,13},{14,15},{16,17},{18,... | collective-permute-start | bytes 1160 | tf_op jit(solution)/shard_map/ppermute | solution.py:21
  125.7 5.5 %collective-permute-start.27 = (f32[10,1,32]{2,1,0:T(1,128)S(1)}, f32[10,1,32]{2,1,0:T(1,128)S(1)}, u32[]{:S(2)}, u32[]{:S(2)}) collective-permute-start(f32[10,1,32]{2,1,0:T(1,128)S(1)} %get-tuple-element.17), channel_id=1, source_target_pairs={{0,1},{2,3},{4,5},{6,7},{8,9},{10,11},{12,13},{14,15},{16,17},{18,... | collective-permute-start | bytes 3848 | tf_op jit(solution)/shard_map/ppermute | solution.py:21
  131.8 4.3 %collective-permute-start.28 = (f32[1,16,64]{2,1,0:T(8,128)S(1)}, f32[1,16,64]{2,1,0:T(8,128)S(1)}, u32[]{:S(2)}, u32[]{:S(2)}) collective-permute-start(f32[1,16,64]{2,1,0:T(8,128)S(1)} %fusion.69), channel_id=1, source_target_pairs={{2,0},{4,2},{6,4},{8,6},{10,8},{12,10},{14,12},{16,14},{18,16},{20... | collective-permute-start | bytes 12296 | tf_op jit(solution)/shard_map/ppermute | solution.py:23
  133.7 5.9 %collective-permute-start.29 = (f32[1,16,64]{2,1,0:T(8,128)S(1)}, f32[1,16,64]{2,1,0:T(8,128)S(1)}, u32[]{:S(2)}, u32[]{:S(2)}) collective-permute-start(f32[1,16,64]{2,1,0:T(8,128)S(1)} %fusion.69), channel_id=1, source_target_pairs={{0,2},{2,4},{4,6},{6,8},{8,10},{10,12},{12,14},{14,16},{16,18},{18... | collective-permute-start | bytes 12296 | tf_op jit(solution)/shard_map/ppermute | solution.py:21
  141.2 5.5 %collective-permute-start.31 = (f32[3,1,64]{2,1,0:T(1,128)S(1)}, f32[3,1,64]{2,1,0:T(1,128)S(1)}, u32[]{:S(2)}, u32[]{:S(2)}) collective-permute-start(f32[3,1,64]{2,1,0:T(1,128)S(1)} %get-tuple-element.29), channel_id=1, source_target_pairs={{0,1},{2,3},{4,5},{6,7},{8,9},{10,11},{12,13},{14,15},{16,17},{18,... | collective-permute-start | bytes 2312 | tf_op jit(solution)/shard_map/ppermute | solution.py:21
  147.1 4.3 %collective-permute-start.32 = (f32[1,32,128]{2,1,0:T(8,128)S(1)}, f32[1,32,128]{2,1,0:T(8,128)S(1)}, u32[]{:S(2)}, u32[]{:S(2)}) collective-permute-start(f32[1,32,128]{2,1,0:T(8,128)S(1)} %get-tuple-element.22), channel_id=1, source_target_pairs={{2,0},{4,2},{6,4},{8,6},{10,8},{12,10},{14,12},{16,14},{18,16},{20... | collective-permute-start | bytes 49160 | tf_op jit(solution)/shard_map/ppermute | solution.py:23
  149.0 6.0 %collective-permute-start.33 = (f32[1,32,128]{2,1,0:T(8,128)S(1)}, f32[1,32,128]{2,1,0:T(8,128)S(1)}, u32[]{:S(2)}, u32[]{:S(2)}) collective-permute-start(f32[1,32,128]{2,1,0:T(8,128)S(1)} %get-tuple-element.21), channel_id=1, source_target_pairs={{0,2},{2,4},{4,6},{6,8},{8,10},{10,12},{12,14},{14,16},{16,18},{18... | collective-permute-start | bytes 49160 | tf_op jit(solution)/shard_map/ppermute | solution.py:21
  156.6 5.5 %collective-permute-start.35 = (f32[4,1,128]{2,1,0:T(1,128)S(1)}, f32[4,1,128]{2,1,0:T(1,128)S(1)}, u32[]{:S(2)}, u32[]{:S(2)}) collective-permute-start(f32[4,1,128]{2,1,0:T(1,128)S(1)} %get-tuple-element.13), channel_id=1, source_target_pairs={{0,1},{2,3},{4,5},{6,7},{8,9},{10,11},{12,13},{14,15},{16,17},{18,... | collective-permute-start | bytes 6152 | tf_op jit(solution)/shard_map/ppermute | solution.py:21
  162.8 4.4 %collective-permute-start.36 = (f32[1,64,256]{1,2,0:T(8,128)S(1)}, f32[1,64,256]{1,2,0:T(8,128)S(1)}, u32[]{:S(2)}, u32[]{:S(2)}) collective-permute-start(f32[1,64,256]{1,2,0:T(8,128)S(1)} %get-tuple-element.10), channel_id=1, source_target_pairs={{2,0},{4,2},{6,4},{8,6},{10,8},{12,10},{14,12},{16,14},{18,16},{20... | collective-permute-start | bytes 196616 | tf_op jit(solution)/shard_map/ppermute | solution.py:23
  164.8 7.2 %collective-permute-start.37 = (f32[1,64,256]{1,2,0:T(8,128)S(1)}, f32[1,64,256]{1,2,0:T(8,128)S(1)}, u32[]{:S(2)}, u32[]{:S(2)}) collective-permute-start(f32[1,64,256]{1,2,0:T(8,128)S(1)} %get-tuple-element.9), channel_id=1, source_target_pairs={{0,2},{2,4},{4,6},{6,8},{8,10},{10,12},{12,14},{14,16},{16,18},{18... | collective-permute-start | bytes 196616 | tf_op jit(solution)/shard_map/ppermute | solution.py:21
  176.5 5.5 %collective-permute-start.39 = (f32[6,1,256]{2,1,0:T(1,128)S(1)}, f32[6,1,256]{2,1,0:T(1,128)S(1)}, u32[]{:S(2)}, u32[]{:S(2)}) collective-permute-start(f32[6,1,256]{2,1,0:T(1,128)S(1)} %copy.97), channel_id=1, source_target_pairs={{0,1},{2,3},{4,5},{6,7},{8,9},{10,11},{12,13},{14,15},{16,17},{18,... | collective-permute-start | bytes 18440 | tf_op jit(solution)/shard_map/ppermute | solution.py:21
  (16 other events, 34.9 us)
where the time goes:
time: 189 us; the launch traced here: 188 us
  waiting for transfers between devices  74.9 us (40%)
  starting transfers between devices  58.3 us (31%)
  local copies, waits for them, and re-layouts  36.3 us (19%)
  other arithmetic  17.1 us (9%)
    ppermute x15, waiting for transfers between devices, padded_2(): lax.ppermute(tail, axis, [(i, (i + 1) % count) for i in range(ends)])  60.4 us
    ppermute x15, starting transfers between devices, padded_2(): lax.ppermute(head, axis, [((i + 1) % count, i) for i in range(ends)])  28 us
    ppermute x15, starting transfers between devices, padded_2(): lax.ppermute(tail, axis, [(i, (i + 1) % count) for i in range(ends)])  25.6 us
    reshape x2, local copies, waits for them, and re-layouts, restrict(): blocks = residual.reshape(size_x // 2, 2, size_y // 2, 2, size_z // 2, 2)  18.4 us
    ppermute x4, waiting for transfers between devices, partner_2(): return lax.ppermute(value, axis, pairs)  13.8 us
    reduce_sum x5, other arithmetic, restrict(): return blocks.sum(axis=(1, 3, 5)) * 0.125  9.96 us
    select_n x1, local copies, waits for them, and re-layouts, body(): jnp.where(upper_half, jnp.concatenate([partner, merged], 0), jnp.concaten...  5.68 us
    ppermute x6, starting transfers between devices, shifted(): return lax.ppermute(shard, axis, pairs)  3.93 us
  transfers between devices with their start and end apart: 40, of which 21 were waited for; matrix products, arithmetic and copies ran while one was open for 1% of the time, Pallas kernels for 0%

commit v1 on v0

v1 whole, which is shorter than its diff:
```python
import functools

import jax
import jax.numpy as jnp
from jax import lax
from jax.experimental import pallas as pl
from jax.experimental.pallas import tpu as pltpu
from jax.sharding import PartitionSpec as P

C = 0.8 / 6.0
CS = 0.8 / 30.0
D1, D2, D3, D4 = C * 4.0, C * 16.0, C * 64.0, C * 256.0
MESH = pl.DeviceIdType.MESH
F32 = jnp.float32
BF16 = jnp.bfloat16


def roll(a, by, axis):
    return pltpu.roll(a, by % a.shape[axis], axis)


def pair_matrix(rows, cols, used_rows, used_cols, down):
    k = lax.broadcasted_iota(jnp.int32, (rows, cols), 0)
    j = lax.broadcasted_iota(jnp.int32, (rows, cols), 1)
    hit = (k // 2 == j) if down else (j // 2 == k)
    hit = hit & (k < used_rows) & (j < used_cols)
    return jnp.where(hit, 1.0, 0.0).astype(BF16)


def split_dot(x, matrix):
    hi = x.astype(BF16)
    rest = x - hi.astype(F32)
    mid = rest.astype(BF16)
    lo = (rest - mid.astype(F32)).astype(BF16)
    out = jnp.dot(hi, matrix, preferred_element_type=F32)
    out = out + jnp.dot(mid, matrix, preferred_element_type=F32)
    return out + jnp.dot(lo, matrix, preferred_element_type=F32)


def z_sum(a, full):
    left, right = roll(a, 1, 1), roll(a, -1, 1)
    if full:
        lane = lax.broadcasted_iota(jnp.int32, a.shape, 1)
        left = jnp.where(lane == 0, 0.0, left)
        right = jnp.where(lane == a.shape[1] - 1, 0.0, right)
    return left + right


def neighbors(a, planes, rows, full, mask_y=True):
    up, down = roll(a, 1, 0), roll(a, -1, 0)
    if mask_y:
        y = lax.broadcasted_iota(jnp.int32, a.shape, 0) % rows
        up = jnp.where(y == 0, 0.0, up)
        down = jnp.where(y == rows - 1, 0.0, down)
    zero = jnp.zeros((rows, a.shape[1]), F32)
    below = jnp.concatenate([zero, a[: (planes - 1) * rows]], 0)
    above = jnp.concatenate([a[rows:], zero], 0)
    return below + above + up + down + z_sum(a, full)


def x_pairs(a, planes, rows):
    return jnp.concatenate(
        [
            a[2 * i * rows : (2 * i + 1) * rows] + a[(2 * i + 1) * rows : (2 * i + 2) * rows]
            for i in range(planes // 2)
        ],
        0,
    )


def kernel(
    n, m, source_ref, obstacle_ref, out_ref,
    sf_ref, xh, yh, ys, r1, gathered, packed, a2, e3s, q2, e2s, e21, e1s, tmp,
    send, recv, gsend, grecv,
):
    gx, gy = lax.axis_index("gx"), lax.axis_index("gy")
    windowed = n > 16
    window = 28 if windowed else 16
    yrows = 16 * m

    def base_of(x):
        return 4 * (x // 4) - 12 if windowed else 0

    base = base_of(gx)

    def peers(fn):
        if not windowed:
            flat = gx * m + gy
            for k in range(1, n * m):
                other = lax.rem(flat + k, n * m)
                fn(other // m, lax.rem(other, m))
            return

        def step(k, carry):
            x, y = base + k // m, lax.rem(k, m)

            @pl.when((x >= 0) & (x < n) & ((x != gx) | (y != gy)))
            def _():
                fn(x, y)

            return carry

        lax.fori_loop(0, window * m, step, 0)

    def exists(dx, dy):
        x, y = gx + dx, gy + dy
        return (x >= 0) & (x < n) & (y >= 0) & (y < m)

    def halo(k, src, dst, dx, dy):
        copy = pltpu.make_async_remote_copy(
            src_ref=src,
            dst_ref=dst,
            send_sem=send.at[k],
            recv_sem=recv.at[k],
            device_id=(jnp.clip(gx + dx, 0, n - 1), jnp.clip(gy + dy, 0, m - 1)),
            device_id_type=MESH,
        )

        def start():
            pl.when(exists(dx, dy))(lambda: copy.start())

        def wait_recv():
            pl.when(exists(-dx, -dy))(lambda: copy.wait_recv())

        def wait_send():
            pl.when(exists(dx, dy))(lambda: copy.wait_send())

        return start, wait_recv, wait_send

    xh[...] = jnp.zeros_like(xh)
    yh[...] = jnp.zeros_like(yh)
    r1[...] = jnp.zeros_like(r1)
    if windowed:
        gathered[...] = jnp.zeros_like(gathered)
    barrier = pltpu.get_barrier_semaphore()

    def greet(x, y):
        pl.semaphore_signal(barrier, inc=1, device_id=(x, y), device_id_type=MESH)

    peers(greet)

    ys[...] = jnp.zeros_like(ys)
    for i in range(4):
        plane = jnp.where(obstacle_ref[i] == 0, source_ref[i], 0.0)
        sf_ref[i] = plane
        ys[0, i : i + 1, :] = plane[0:1]
        ys[1, i : i + 1, :] = plane[63:64]
    e3s[...] = jnp.zeros_like(e3s)
    e2s[...] = jnp.zeros_like(e2s)
    a2[...] = jnp.zeros_like(a2)

    if not windowed:
        pl.semaphore_wait(barrier, n * m - 1)
    else:
        peers(lambda x, y: pl.semaphore_wait(barrier, 1))

    halos = []

    def add(src, dst, dx, dy):
        halos.append(halo(len(halos), src, dst, dx, dy))
        return halos[-1]

    first = [
        add(sf_ref.at[3], xh.at[0], 1, 0),
        add(sf_ref.at[0], xh.at[1], -1, 0),
        add(ys.at[1], yh.at[0], 0, 1),
        add(ys.at[0], yh.at[1], 0, -1),
    ]
    for start, _, _ in first:
        start()

    row = lax.broadcasted_iota(jnp.int32, (64, 256), 0)

    def fine_neighbors(planes, i, above_row, below_row):
        p = planes[i + 1]
        up = jnp.where(row == 0, above_row, roll(p, 1, 0))
        down = jnp.where(row == 63, below_row, roll(p, -1, 0))
        return planes[i] + planes[i + 2] + up + down + z_sum(p, True)

    for _, wait, _ in first:
        wait()
    planes = [xh[0]] + [sf_ref[i] for i in range(4)] + [xh[1]]
    left = [
        0.2 * planes[i + 1]
        + C * fine_neighbors(planes, i, yh[0, i : i + 1, :], yh[1, i : i + 1, :])
        for i in range(4)
    ]
    summed = jnp.concatenate([left[0] + left[1], left[2] + left[3]], 0)
    tmp[0:128] = split_dot(summed, pair_matrix(256, 128, 256, 128, True)) * 0.125
    for i in range(2):
        own = tmp[pl.ds(64 * i, 32, stride=2), :] + tmp[pl.ds(64 * i + 1, 32, stride=2), :]
        r1[2 + i, 8:40, :] = own

    mid = pl.ds(8, 32)
    second = [
        add(r1.at[3, mid], r1.at[1, mid], 1, 0),
        add(r1.at[2, mid], r1.at[4, mid], -1, 0),
        add(r1.at[pl.ds(2, 2), pl.ds(32, 8)], r1.at[pl.ds(2, 2), pl.ds(0, 8)], 0, 1),
        add(r1.at[pl.ds(2, 2), pl.ds(8, 8)], r1.at[pl.ds(2, 2), pl.ds(40, 8)], 0, -1),
    ]
    third = [
        add(r1.at[2, mid], r1.at[0, mid], 1, 0),
        add(r1.at[3, mid], r1.at[5, mid], -1, 0),
        add(r1.at[3, pl.ds(32, 8)], r1.at[1, pl.ds(0, 8)], 1, 1),
        add(r1.at[3, pl.ds(8, 8)], r1.at[1, pl.ds(40, 8)], 1, -1),
        add(r1.at[2, pl.ds(32, 8)], r1.at[4, pl.ds(0, 8)], -1, 1),
        add(r1.at[2, pl.ds(8, 8)], r1.at[4, pl.ds(40, 8)], -1, -1),
    ]
    for start, _, _ in second + third:
        start()
    for _, wait, _ in second:
        wait()

    near = [r1[k, 8:40, :] for k in range(1, 5)]
    left1 = []
    for i in (1, 2):
        p = r1[i + 1]
        total = (roll(p, 1, 0) + roll(p, -1, 0) + z_sum(p, True))[8:40]
        left1.append(0.2 * near[i] + C * (near[i - 1] + near[i + 1] + total))
    tmp[0:32] = split_dot(left1[0] + left1[1], pair_matrix(128, 128, 128, 64, True)) * 0.125
    r2 = tmp[pl.ds(0, 16, stride=2), :] + tmp[pl.ds(1, 16, stride=2), :]
    mine = r2[0:8] + roll(r2[8:16], 64, 1)
    packed[...] = mine
    gathered[(gx - base) * m + gy] = mine

    def tile_copy(x, y):
        return pltpu.make_async_remote_copy(
            src_ref=packed,
            dst_ref=gathered.at[(gx - base_of(x)) * m + gy],
            send_sem=gsend,
            recv_sem=grecv,
            device_id=(x, y),
            device_id_type=MESH,
        )

    peers(lambda x, y: tile_copy(x, y).start())
    if not windowed:
        many = gathered.at[pl.ds(0, n * m - 1)]
        pltpu.make_async_copy(many, many, grecv).wait()
    else:
        peers(lambda x, y: tile_copy(x, y).wait_recv())

    def inside(a, planes, rows, first_plane, count):
        if not windowed:
            return a
        x = first_plane + lax.broadcasted_iota(jnp.int32, a.shape, 0) // rows
        return jnp.where((x >= 0) & (x < count), a, 0.0)

    tiles = gathered[...].reshape(window * m * 8, 128)
    lane = lax.broadcasted_iota(jnp.int32, tiles.shape, 1)
    low = jnp.where(lane < 64, tiles, 0.0).reshape(window * m, 8, 128)
    high = jnp.where(lane < 64, roll(tiles, 64, 1), 0.0).reshape(window * m, 8, 128)
    a2[pl.ds(2 * m, window * m), 0:8, :] = low
    a2[pl.ds(2 * m, window * m), 8:16, :] = high
    full2 = a2[pl.ds(2 * m, window * m)].reshape(window * yrows, 128)

    def restrict(a, planes, rows, used):
        count = planes // 2 * rows
        folded = x_pairs(a, planes, rows)
        tmp[0:count] = split_dot(folded, pair_matrix(128, 128, used, used // 2, True)) * 0.125
        half = count // 2
        return tmp[pl.ds(0, half, stride=2), :] + tmp[pl.ds(1, half, stride=2), :]

    def prolong_yz(a, used, dst):
        wide = split_dot(a, pair_matrix(128, 128, used, used * 2, False))
        dst[pl.ds(0, a.shape[0], stride=2), :] = wide
        dst[pl.ds(1, a.shape[0], stride=2), :] = wide

    x3, y3 = window // 2, yrows // 2
    x4, y4 = window // 4, yrows // 4
    r3 = restrict(0.2 * full2 + C * neighbors(full2, window, yrows, False), window, yrows, 64)
    r4 = restrict(0.2 * r3 + C * neighbors(r3, x3, y3, False), x3, y3, 32)
    e4 = D4 * (1.2 * r4 + C * neighbors(r4, x4, y4, False))
    e4 = inside(e4, x4, y4, base // 4, n // 4)
    prolong_yz(e4, 16, tmp)
    e3 = D3 * r3 + jnp.concatenate(
        [tmp[pl.ds((i // 2) * y3, y3), :] for i in range(x3)], 0
    )
    e3 = 0.2 * e3 + D3 * r3 + C * neighbors(e3, x3, y3, False)
    e3 = inside(e3, x3, y3, base // 2, n // 2)
    e3s[pl.ds(1, x3)] = e3.reshape(x3, y3, 128)

    low3 = (gx - base + 2) // 2 - 1
    prolong_yz(e3s[pl.ds(low3, 3)].reshape(3 * y3, 128), 32, q2)
    odd = lax.rem(gx, 2)
    rs, es = [], []
    for d in range(-2, 3):
        plane = a2[pl.ds((gx - base + 2 + d) * m, m)].reshape(yrows, 128)
        start = pl.multiple_of(((odd + d + 2) // 2) * yrows, 8)
        rs.append(plane)
        es.append(D2 * plane + q2[pl.ds(start, yrows), :])
    rs, es = jnp.concatenate(rs, 0), jnp.concatenate(es, 0)
    e2 = 0.2 * es + D2 * rs + C * neighbors(es, 5, yrows, False)
    e2 = e2[yrows : 4 * yrows]
    wide = split_dot(e2, pair_matrix(128, 128, 64, 128, False))
    alive = [jnp.where(gx > 0, 1.0, 0.0), 1.0, jnp.where(gx < n - 1, 1.0, 0.0)]
    for i in range(3):
        e2s[i, pl.ds(8, yrows), :] = wide[i * yrows : (i + 1) * yrows] * alive[i]
    for i in range(3):
        part = e2s[i, pl.ds(gy * 16 + 4, 24), :]
        e21[pl.ds(48 * i, 24, stride=2), :] = part
        e21[pl.ds(48 * i + 1, 24, stride=2), :] = part

    for _, wait, _ in third:
        wait()
    r1s = [r1[k] for k in range(6)]
    e1p = [D1 * r1s[k] + e21[48 * (k // 2) : 48 * (k // 2) + 48, :] for k in range(6)]
    y = gy * 32 - 8 + lax.broadcasted_iota(jnp.int32, (48, 128), 0)
    y_in = (y >= 0) & (y < 32 * m)
    done = []
    for k in range(1, 5):
        p = e1p[k]
        total = e1p[k - 1] + e1p[k + 1] + roll(p, 1, 0) + roll(p, -1, 0) + z_sum(p, True)
        value = jnp.where(y_in, 0.2 * p + D1 * r1s[k] + C * total, 0.0)
        if k == 1:
            value = value * alive[0]
        if k == 4:
            value = value * alive[2]
        done.append(value)
    done = jnp.concatenate(done, 0)
    wide = split_dot(done, pair_matrix(128, 256, 128, 256, False))
    for h in range(2):
        half = wide[:, 128 * h : 128 * h + 128]
        e1s[h, pl.ds(0, 192, stride=2), :] = half
        e1s[h, pl.ds(1, 192, stride=2), :] = half

    def coarse(k, start, rows):
        return jnp.concatenate([e1s[h, 96 * k + start : 96 * k + start + rows, :] for h in (0, 1)], 1)

    blocks = [coarse(k, 16, 64) for k in range(4)]
    planes = [C * xh[0] + blocks[0]]
    planes += [C * sf_ref[i] + blocks[1 + i // 2] for i in range(4)]
    planes += [C * xh[1] + blocks[3]]
    for i in range(4):
        k = 1 + i // 2
        above = C * yh[0, i : i + 1, :] + coarse(k, 15, 1)
        below = C * yh[1, i : i + 1, :] + coarse(k, 80, 1)
        total = fine_neighbors(planes, i, above, below)
        weight = jnp.where(obstacle_ref[i] == 0, C, CS)
        out_ref[i] = 0.2 * planes[i + 1] + weight * (sf_ref[i] + total)

    for _, _, wait in halos:
        wait()
    if not windowed:
        many = gathered.at[pl.ds(0, n * m - 1)]
        pltpu.make_async_copy(many, many, gsend).wait()
    else:
        peers(lambda x, y: tile_copy(x, y).wait_send())


def solution(mesh):
    n, m = mesh.shape["gx"], mesh.shape["gy"]
    window = 28 if n > 16 else 16
    rows = 16 * m

    def body(source, obstacle):
        vmem = pl.BlockSpec(memory_space=pltpu.VMEM)
        return pl.pallas_call(
            functools.partial(kernel, n, m),
            out_shape=jax.ShapeDtypeStruct(source.shape, F32),
            in_specs=[vmem, vmem],
            out_specs=vmem,
            scratch_shapes=[
                pltpu.VMEM((4, 64, 256), F32),
                pltpu.VMEM((2, 64, 256), F32),
                pltpu.VMEM((2, 8, 256), F32),
                pltpu.VMEM((2, 8, 256), F32),
                pltpu.VMEM((6, 48, 128), F32),
                pltpu.VMEM((window * m, 8, 128), F32),
                pltpu.VMEM((8, 128), F32),
                pltpu.VMEM(((window + 4) * m, 16, 128), F32),
                pltpu.VMEM((window // 2 + 2, rows // 2, 128), F32),
                pltpu.VMEM((3 * rows, 128), F32),
                pltpu.VMEM((3, rows + 16, 128), F32),
                pltpu.VMEM((144, 128), F32),
                pltpu.VMEM((2, 384, 128), F32),
                pltpu.VMEM((max(128, window // 2 * rows), 128), F32),
                pltpu.SemaphoreType.DMA((14,)),
                pltpu.SemaphoreType.DMA((14,)),
                pltpu.SemaphoreType.DMA,
                pltpu.SemaphoreType.DMA,
            ],
            compiler_params=pltpu.CompilerParams(
                collective_id=0, has_side_effects=True, vmem_limit_bytes=32 * 1024 * 1024
            ),
        )(source, obstacle)

    spec = P("gx", "gy", None)
    return jax.shard_map(
        body, mesh=mesh, in_specs=(spec, spec), out_specs=spec, check_vma=False
    )
```

time: 189 us -> 21.8 us (0.12)
  the two profiles are of different devices: /device:TPU:26 before, /device:TPU:1 now
where the time goes in v1:
time: 21.8 us; the launch traced here: 21.6 us
  Pallas kernels  19 us (87%)
  local copies, waits for them, and re-layouts  2.6 us (12%)
    pallas_call x1, Pallas kernels, body(): pl.pallas_call(functools.partial(kernel, n, m), out_shape=jax.ShapeDtypeS...  19 us
    unnamed x5, local copies, waits for them, and re-layouts  2.6 us

profile of v1, /device:TPU:1, one launch (start us, length us, event | category | flops | bytes accessed | tf_op | source)
XLA Modules:
  0.0 21.6 jit_solution(7792575164007268064)
XLA Ops:
  0.0 0.0 copy-start
  0.0 0.9 %copy-done = f32[4,64,256]{2,1,0:T(8,128)S(1)} copy-done((f32[4,64,256]{2,1,0:T(8,128)S(1)}, f32[4,64,256]{2,1,0:T(8,128)}, u32[]{:S(2)}) %copy-start) | copy-done | bytes 262168
  1.0 0.0 copy-start.1
  1.0 0.9 %copy-done.1 = s32[4,64,256]{2,1,0:T(8,128)S(1)} copy-done((s32[4,64,256]{2,1,0:T(8,128)S(1)}, s32[4,64,256]{2,1,0:T(8,128)}, u32[]{:S(2)}) %copy-start.1) | copy-done | bytes 262168
  1.9 19.0 %shard_map.28 = f32[4,64,256]{2,1,0:T(8,128)S(1)} custom-call(f32[4,64,256]{2,1,0:T(8,128)S(1)} %copy-done, s32[4,64,256]{2,1,0:T(8,128)S(1)} %copy-done.1), custom_call_target="tpu_custom_call" | custom-call | tf_op jit(solution)/shard_map/pallas_call | solution.py:358
  20.9 0.7 %copy.4 = f32[4,64,256]{2,1,0:T(8,128)} copy(f32[4,64,256]{2,1,0:T(8,128)S(1)} %shard_map.28) | data formatting | bytes 524288
Async XLA Ops:
  0.0 0.9 %copy-start = (f32[4,64,256]{2,1,0:T(8,128)S(1)}, f32[4,64,256]{2,1,0:T(8,128)}, u32[]{:S(2)}) copy-start(f32[4,64,256]{2,1,0:T(8,128)} %source_ref.1) | copy-start | bytes 786436
  1.0 0.9 %copy-start.1 = (s32[4,64,256]{2,1,0:T(8,128)S(1)}, s32[4,64,256]{2,1,0:T(8,128)}, u32[]{:S(2)}) copy-start(s32[4,64,256]{2,1,0:T(8,128)} %obstacle_ref.1) | copy-start | bytes 786436

commit v2 on v1

--- a/solution.py
+++ b/solution.py
@@ -49,7 +49,8 @@
 def neighbors(a, planes, rows, full, mask_y=True):
     up, down = roll(a, 1, 0), roll(a, -1, 0)
     if mask_y:
-        y = lax.broadcasted_iota(jnp.int32, a.shape, 0) % rows
+        y = lax.broadcasted_iota(jnp.int32, a.shape, 0)
+        y = y & (rows - 1) if rows & (rows - 1) == 0 else y % rows
         up = jnp.where(y == 0, 0.0, up)
         down = jnp.where(y == rows - 1, 0.0, down)
     zero = jnp.zeros((rows, a.shape[1]), F32)
@@ -70,8 +71,8 @@
 
 def kernel(
     n, m, source_ref, obstacle_ref, out_ref,
-    sf_ref, xh, yh, ys, r1, gathered, packed, a2, e3s, q2, e2s, e21, e1s, tmp,
-    send, recv, gsend, grecv,
+    src, obs, sf_ref, xh, yh, ys, r1, gathered, packed, a2, e3s, q2, e2s, e21, e1s, tmp,
+    send, recv, gsend, grecv, load,
 ):
     gx, gy = lax.axis_index("gx"), lax.axis_index("gy")
     windowed = n > 16
@@ -127,6 +128,12 @@
 
         return start, wait_recv, wait_send
 
+    loads = [
+        pltpu.make_async_copy(source_ref, src, load.at[0]),
+        pltpu.make_async_copy(obstacle_ref, obs, load.at[1]),
+    ]
+    for copy in loads:
+        copy.start()
     xh[...] = jnp.zeros_like(xh)
     yh[...] = jnp.zeros_like(yh)
     r1[...] = jnp.zeros_like(r1)
@@ -140,14 +147,16 @@
     peers(greet)
 
     ys[...] = jnp.zeros_like(ys)
+    e3s[...] = jnp.zeros_like(e3s)
+    e2s[...] = jnp.zeros_like(e2s)
+    a2[...] = jnp.zeros_like(a2)
+    for copy in loads:
+        copy.wait()
     for i in range(4):
-        plane = jnp.where(obstacle_ref[i] == 0, source_ref[i], 0.0)
+        plane = jnp.where(obs[i] == 0, src[i], 0.0)
         sf_ref[i] = plane
         ys[0, i : i + 1, :] = plane[0:1]
         ys[1, i : i + 1, :] = plane[63:64]
-    e3s[...] = jnp.zeros_like(e3s)
-    e2s[...] = jnp.zeros_like(e2s)
-    a2[...] = jnp.zeros_like(a2)
 
     if not windowed:
         pl.semaphore_wait(barrier, n * m - 1)
@@ -336,7 +345,7 @@
         above = C * yh[0, i : i + 1, :] + coarse(k, 15, 1)
         below = C * yh[1, i : i + 1, :] + coarse(k, 80, 1)
         total = fine_neighbors(planes, i, above, below)
-        weight = jnp.where(obstacle_ref[i] == 0, C, CS)
+        weight = jnp.where(obs[i] == 0, C, CS)
         out_ref[i] = 0.2 * planes[i + 1] + weight * (sf_ref[i] + total)
 
     for _, _, wait in halos:
@@ -358,9 +367,11 @@
         return pl.pallas_call(
             functools.partial(kernel, n, m),
             out_shape=jax.ShapeDtypeStruct(source.shape, F32),
-            in_specs=[vmem, vmem],
+            in_specs=[pl.BlockSpec(memory_space=pltpu.HBM)] * 2,
             out_specs=vmem,
             scratch_shapes=[
+                pltpu.VMEM(source.shape, F32),
+                pltpu.VMEM(source.shape, jnp.int32),
                 pltpu.VMEM((4, 64, 256), F32),
                 pltpu.VMEM((2, 64, 256), F32),
                 pltpu.VMEM((2, 8, 256), F32),
@@ -379,6 +390,7 @@
                 pltpu.SemaphoreType.DMA((14,)),
                 pltpu.SemaphoreType.DMA,
                 pltpu.SemaphoreType.DMA,
+                pltpu.SemaphoreType.DMA((2,)),
             ],
             compiler_params=pltpu.CompilerParams(
                 collective_id=0, has_side_effects=True, vmem_limit_bytes=32 * 1024 * 1024

time: 21.8 us -> 21.8 us (level)
  no operation moved by 1% of the time
where the time goes in v2:
time: 21.8 us; the launch traced here: 21.6 us
  Pallas kernels  19 us (87%)
  local copies, waits for them, and re-layouts  2.6 us (12%)
    pallas_call x1, Pallas kernels, body(): pl.pallas_call(functools.partial(kernel, n, m), out_shape=jax.ShapeDtypeS...  19 us
    unnamed x5, local copies, waits for them, and re-layouts  2.6 us

profile of v2, /device:TPU:1, one launch (start us, length us, event | category | flops | bytes accessed | tf_op | source)
XLA Modules:
  0.0 21.6 jit_solution(18315753528992428282)
XLA Ops:
  0.0 0.0 copy-start
  0.0 0.9 %copy-done = f32[4,64,256]{2,1,0:T(8,128)S(1)} copy-done((f32[4,64,256]{2,1,0:T(8,128)S(1)}, f32[4,64,256]{2,1,0:T(8,128)}, u32[]{:S(2)}) %copy-start) | copy-done | bytes 262168
  1.0 0.0 copy-start.1
  1.0 0.9 %copy-done.1 = s32[4,64,256]{2,1,0:T(8,128)S(1)} copy-done((s32[4,64,256]{2,1,0:T(8,128)S(1)}, s32[4,64,256]{2,1,0:T(8,128)}, u32[]{:S(2)}) %copy-start.1) | copy-done | bytes 262168
  1.9 19.0 %shard_map.28 = f32[4,64,256]{2,1,0:T(8,128)S(1)} custom-call(f32[4,64,256]{2,1,0:T(8,128)S(1)} %copy-done, s32[4,64,256]{2,1,0:T(8,128)S(1)} %copy-done.1), custom_call_target="tpu_custom_call" | custom-call | tf_op jit(solution)/shard_map/pallas_call | solution.py:367
  20.9 0.7 %copy.4 = f32[4,64,256]{2,1,0:T(8,128)} copy(f32[4,64,256]{2,1,0:T(8,128)S(1)} %shard_map.28) | data formatting | bytes 524288
Async XLA Ops:
  0.0 0.9 %copy-start = (f32[4,64,256]{2,1,0:T(8,128)S(1)}, f32[4,64,256]{2,1,0:T(8,128)}, u32[]{:S(2)}) copy-start(f32[4,64,256]{2,1,0:T(8,128)} %source_ref.1) | copy-start | bytes 786436
  1.0 0.9 %copy-start.1 = (s32[4,64,256]{2,1,0:T(8,128)S(1)}, s32[4,64,256]{2,1,0:T(8,128)}, u32[]{:S(2)}) copy-start(s32[4,64,256]{2,1,0:T(8,128)} %obstacle_ref.1) | copy-start | bytes 786436

commit v3 on v2

--- a/solution.py
+++ b/solution.py
@@ -71,8 +71,8 @@
 
 def kernel(
     n, m, source_ref, obstacle_ref, out_ref,
-    src, obs, sf_ref, xh, yh, ys, r1, gathered, packed, a2, e3s, q2, e2s, e21, e1s, tmp,
-    send, recv, gsend, grecv, load,
+    src, obs, xs, xr, y_out, y_in_ref, d_out, d_in, sf_ref, xh, yh, ys, r1, gathered, packed, a2, e3s, q2, e2s, e21, e1s, tmp,
+    send, recv, gsend, grecv, load, ready,
 ):
     gx, gy = lax.axis_index("gx"), lax.axis_index("gy")
     windowed = n > 16
@@ -137,6 +137,9 @@
     xh[...] = jnp.zeros_like(xh)
     yh[...] = jnp.zeros_like(yh)
     r1[...] = jnp.zeros_like(r1)
+    xr[...] = jnp.zeros_like(xr)
+    y_in_ref[...] = jnp.zeros_like(y_in_ref)
+    d_in[...] = jnp.zeros_like(d_in)
     if windowed:
         gathered[...] = jnp.zeros_like(gathered)
     barrier = pltpu.get_barrier_semaphore()
@@ -144,9 +147,41 @@
     def greet(x, y):
         pl.semaphore_signal(barrier, inc=1, device_id=(x, y), device_id_type=MESH)
 
-    peers(greet)
+    group = n * m // 4
+    flat = gx * m + gy
+
+    def counterparts(fn):
+        for k in range(1, 4):
+            other = lax.rem(flat + k * group, n * m)
+            fn(other // m, lax.rem(other, m))
+
+    def across(fn=None):
+        count = 0
+        for dx in (-1, 1):
+            for dy in range(-1, 2):
+                x, y = gx + dx, gy + dy
+                fits = exists(dx, dy) & ((x * m + y) // group != flat // group)
+                fits = fits & (lax.rem(x * m + y - flat + n * m, group) != 0)
+                if fn is None:
+                    count = count + jnp.where(fits, 1, 0)
+                else:
+                    pl.when(fits)(lambda x=x, y=y: fn(x, y))
+        return count
+
+    def first_stage(fn):
+        if windowed:
+            return peers(fn)
+        for k in range(1, group):
+            other = flat // group * group + lax.rem(flat + k, group)
+            fn(other // m, lax.rem(other, m))
+        counterparts(fn)
+        across(fn)
+
+    first_stage(greet)
 
     ys[...] = jnp.zeros_like(ys)
+    y_out[...] = jnp.zeros_like(y_out)
+    d_out[...] = jnp.zeros_like(d_out)
     e3s[...] = jnp.zeros_like(e3s)
     e2s[...] = jnp.zeros_like(e2s)
     a2[...] = jnp.zeros_like(a2)
@@ -158,10 +193,19 @@
         ys[0, i : i + 1, :] = plane[0:1]
         ys[1, i : i + 1, :] = plane[63:64]
 
-    if not windowed:
-        pl.semaphore_wait(barrier, n * m - 1)
+    if windowed:
+        total = 0
+        for k in range(window * m):
+            x, y = base + k // m, k % m
+            total = total + jnp.where((x >= 0) & (x < n) & ((x != gx) | (y != gy)), 1, 0)
+        pl.semaphore_wait(barrier, total)
     else:
-        peers(lambda x, y: pl.semaphore_wait(barrier, 1))
+        pl.semaphore_wait(barrier, group + 2 + across())
+        counterparts(
+            lambda x, y: pl.semaphore_signal(
+                ready, inc=1, device_id=(x, y), device_id_type=MESH
+            )
+        )
 
     halos = []
 
@@ -169,16 +213,9 @@
         halos.append(halo(len(halos), src, dst, dx, dy))
         return halos[-1]
 
-    first = [
-        add(sf_ref.at[3], xh.at[0], 1, 0),
-        add(sf_ref.at[0], xh.at[1], -1, 0),
-        add(ys.at[1], yh.at[0], 0, 1),
-        add(ys.at[0], yh.at[1], 0, -1),
-    ]
-    for start, _, _ in first:
-        start()
-
+    zmat = pair_matrix(256, 128, 256, 128, True)
     row = lax.broadcasted_iota(jnp.int32, (64, 256), 0)
+    row1 = lax.broadcasted_iota(jnp.int32, (32, 128), 0)
 
     def fine_neighbors(planes, i, above_row, below_row):
         p = planes[i + 1]
@@ -186,46 +223,74 @@
         down = jnp.where(row == 63, below_row, roll(p, -1, 0))
         return planes[i] + planes[i + 2] + up + down + z_sum(p, True)
 
+    zero = jnp.zeros((64, 256), F32)
+    fine = [sf_ref[i] for i in range(4)]
+    padded = [zero] + fine + [zero]
+    left = [0.2 * fine[i] + C * fine_neighbors(padded, i, 0.0, 0.0) for i in range(4)]
+    rim = [C * (fine[2 * i][r : r + 1] + fine[2 * i + 1][r : r + 1]) for i in (0, 1) for r in (0, 63)]
+    rows_in = [left[0] + left[1], left[2] + left[3], C * fine[0], C * fine[3]]
+    rows_in += rim + [jnp.zeros((4, 256), F32)]
+    tmp[0:264] = split_dot(jnp.concatenate(rows_in, 0), zmat) * 0.125
+    part0, part1, side0, side1 = [
+        tmp[pl.ds(64 * i, 32, stride=2), :] + tmp[pl.ds(64 * i + 1, 32, stride=2), :]
+        for i in range(4)
+    ]
+    edge = [[tmp[256 + 2 * i + r : 257 + 2 * i + r, :] for r in (0, 1)] for i in (0, 1)]
+    parts, sides = (part0, part1), (side0, side1)
+    for i in (0, 1):
+        xs[i, 0] = parts[i]
+        xs[i, 1] = sides[i]
+    for r in (0, 1):
+        cut = slice(31 * r, 31 * r + 1)
+        for i in (0, 1):
+            y_out[r, i : i + 1, :] = parts[i][cut]
+            y_out[r, 2 + i : 3 + i, :] = edge[i][r]
+            d_out[2 * i + r, 0:1, :] = edge[i][r]
+            d_out[2 * i + r, 1:2, :] = sides[i][cut]
+    first = [
+        add(xs.at[1], xr.at[0], 1, 0),
+        add(xs.at[0], xr.at[1], -1, 0),
+        add(y_out.at[1], y_in_ref.at[0], 0, 1),
+        add(y_out.at[0], y_in_ref.at[1], 0, -1),
+        add(d_out.at[3], d_in.at[0], 1, 1),
+        add(d_out.at[2], d_in.at[1], 1, -1),
+        add(d_out.at[1], d_in.at[2], -1, 1),
+        add(d_out.at[0], d_in.at[3], -1, -1),
+    ]
+    for start, _, _ in first:
+        start()
     for _, wait, _ in first:
         wait()
-    planes = [xh[0]] + [sf_ref[i] for i in range(4)] + [xh[1]]
-    left = [
-        0.2 * planes[i + 1]
-        + C * fine_neighbors(planes, i, yh[0, i : i + 1, :], yh[1, i : i + 1, :])
-        for i in range(4)
+
+    def with_edges(a, top, bottom):
+        a = a + jnp.where(row1 == 0, top, 0.0)
+        return a + jnp.where(row1 == 31, bottom, 0.0)
+
+    alive = [jnp.where(gx > 0, 1.0, 0.0), 1.0, jnp.where(gx < n - 1, 1.0, 0.0)]
+    own = []
+    for i in (0, 1):
+        a = parts[i] + xr[i, 1]
+        own.append(with_edges(a, y_in_ref[0, 2 + i : 3 + i, :], y_in_ref[1, 2 + i : 3 + i, :]))
+    beside = []
+    for i in (0, 1):
+        a = xr[i, 0] + sides[i]
+        a = with_edges(a, d_in[2 * i, 0:1, :], d_in[2 * i + 1, 0:1, :])
+        beside.append(a * alive[2 * i])
+    y_alive = [jnp.where(gy > 0, 1.0, 0.0), jnp.where(gy < m - 1, 1.0, 0.0)]
+    rim1 = [
+        [
+            y_alive[r] * (y_in_ref[r, i : i + 1, :] + edge[i][r] + d_in[2 * i + r, 1:2, :])
+            for r in (0, 1)
+        ]
+        for i in (0, 1)
     ]
-    summed = jnp.concatenate([left[0] + left[1], left[2] + left[3]], 0)
-    tmp[0:128] = split_dot(summed, pair_matrix(256, 128, 256, 128, True)) * 0.125
-    for i in range(2):
-        own = tmp[pl.ds(64 * i, 32, stride=2), :] + tmp[pl.ds(64 * i + 1, 32, stride=2), :]
-        r1[2 + i, 8:40, :] = own
-
-    mid = pl.ds(8, 32)
-    second = [
-        add(r1.at[3, mid], r1.at[1, mid], 1, 0),
-        add(r1.at[2, mid], r1.at[4, mid], -1, 0),
-        add(r1.at[pl.ds(2, 2), pl.ds(32, 8)], r1.at[pl.ds(2, 2), pl.ds(0, 8)], 0, 1),
-        add(r1.at[pl.ds(2, 2), pl.ds(8, 8)], r1.at[pl.ds(2, 2), pl.ds(40, 8)], 0, -1),
-    ]
-    third = [
-        add(r1.at[2, mid], r1.at[0, mid], 1, 0),
-        add(r1.at[3, mid], r1.at[5, mid], -1, 0),
-        add(r1.at[3, pl.ds(32, 8)], r1.at[1, pl.ds(0, 8)], 1, 1),
-        add(r1.at[3, pl.ds(8, 8)], r1.at[1, pl.ds(40, 8)], 1, -1),
-        add(r1.at[2, pl.ds(32, 8)], r1.at[4, pl.ds(0, 8)], -1, 1),
-        add(r1.at[2, pl.ds(8, 8)], r1.at[4, pl.ds(40, 8)], -1, -1),
-    ]
-    for start, _, _ in second + third:
-        start()
-    for _, wait, _ in second:
-        wait()
-
-    near = [r1[k, 8:40, :] for k in range(1, 5)]
     left1 = []
-    for i in (1, 2):
-        p = r1[i + 1]
-        total = (roll(p, 1, 0) + roll(p, -1, 0) + z_sum(p, True))[8:40]
-        left1.append(0.2 * near[i] + C * (near[i - 1] + near[i + 1] + total))
+    for i in (0, 1):
+        p = own[i]
+        up = jnp.where(row1 == 0, rim1[i][0], roll(p, 1, 0))
+        down = jnp.where(row1 == 31, rim1[i][1], roll(p, -1, 0))
+        total = beside[i] + own[1 - i] + up + down + z_sum(p, True)
+        left1.append(0.2 * p + C * total)
     tmp[0:32] = split_dot(left1[0] + left1[1], pair_matrix(128, 128, 128, 64, True)) * 0.125
     r2 = tmp[pl.ds(0, 16, stride=2), :] + tmp[pl.ds(1, 16, stride=2), :]
     mine = r2[0:8] + roll(r2[8:16], 64, 1)
@@ -242,7 +307,29 @@
             device_id_type=MESH,
         )
 
+    if not windowed:
+        pl.semaphore_wait(ready, 3)
     peers(lambda x, y: tile_copy(x, y).start())
+    for i in (0, 1):
+        r1[2 + i, 8:40, :] = own[i]
+        r1[1 + 3 * i, 8:40, :] = beside[i]
+    mid = pl.ds(8, 32)
+    third = [
+        add(r1.at[2, mid], r1.at[0, mid], 1, 0),
+        add(r1.at[3, mid], r1.at[5, mid], -1, 0),
+        add(r1.at[pl.ds(2, 2), pl.ds(32, 8)], r1.at[pl.ds(2, 2), pl.ds(0, 8)], 0, 1),
+        add(r1.at[pl.ds(2, 2), pl.ds(8, 8)], r1.at[pl.ds(2, 2), pl.ds(40, 8)], 0, -1),
+        add(r1.at[3, pl.ds(32, 8)], r1.at[1, pl.ds(0, 8)], 1, 1),
+        add(r1.at[3, pl.ds(8, 8)], r1.at[1, pl.ds(40, 8)], 1, -1),
+        add(r1.at[2, pl.ds(32, 8)], r1.at[4, pl.ds(0, 8)], -1, 1),
+        add(r1.at[2, pl.ds(8, 8)], r1.at[4, pl.ds(40, 8)], -1, -1),
+        add(sf_ref.at[3], xh.at[0], 1, 0),
+        add(sf_ref.at[0], xh.at[1], -1, 0),
+        add(ys.at[1], yh.at[0], 0, 1),
+        add(ys.at[0], yh.at[1], 0, -1),
+    ]
+    for start, _, _ in third:
+        start()
     if not windowed:
         many = gathered.at[pl.ds(0, n * m - 1)]
         pltpu.make_async_copy(many, many, grecv).wait()
@@ -302,7 +389,6 @@
     e2 = 0.2 * es + D2 * rs + C * neighbors(es, 5, yrows, False)
     e2 = e2[yrows : 4 * yrows]
     wide = split_dot(e2, pair_matrix(128, 128, 64, 128, False))
-    alive = [jnp.where(gx > 0, 1.0, 0.0), 1.0, jnp.where(gx < n - 1, 1.0, 0.0)]
     for i in range(3):
         e2s[i, pl.ds(8, yrows), :] = wide[i * yrows : (i + 1) * yrows] * alive[i]
     for i in range(3):
@@ -372,6 +458,12 @@
             scratch_shapes=[
                 pltpu.VMEM(source.shape, F32),
                 pltpu.VMEM(source.shape, jnp.int32),
+                pltpu.VMEM((2, 2, 32, 128), F32),
+                pltpu.VMEM((2, 2, 32, 128), F32),
+                pltpu.VMEM((2, 8, 128), F32),
+                pltpu.VMEM((2, 8, 128), F32),
+                pltpu.VMEM((4, 8, 128), F32),
+                pltpu.VMEM((4, 8, 128), F32),
                 pltpu.VMEM((4, 64, 256), F32),
                 pltpu.VMEM((2, 64, 256), F32),
                 pltpu.VMEM((2, 8, 256), F32),
@@ -385,12 +477,13 @@
                 pltpu.VMEM((3, rows + 16, 128), F32),
                 pltpu.VMEM((144, 128), F32),
                 pltpu.VMEM((2, 384, 128), F32),
-                pltpu.VMEM((max(128, window // 2 * rows), 128), F32),
-                pltpu.SemaphoreType.DMA((14,)),
-                pltpu.SemaphoreType.DMA((14,)),
+                pltpu.VMEM((max(264, window // 2 * rows), 128), F32),
+                pltpu.SemaphoreType.DMA((20,)),
+                pltpu.SemaphoreType.DMA((20,)),
                 pltpu.SemaphoreType.DMA,
                 pltpu.SemaphoreType.DMA,
                 pltpu.SemaphoreType.DMA((2,)),
+                pltpu.SemaphoreType.REGULAR,
             ],
             compiler_params=pltpu.CompilerParams(
                 collective_id=0, has_side_effects=True, vmem_limit_bytes=32 * 1024 * 1024

time: 21.8 us -> 19.1 us (0.88)
  Pallas kernels: 19 us -> 16.1 us
    pallas_call x1, Pallas kernels: 19 us -> 16.1 us  [body(): pl.pallas_call(functools.partial(kernel, n, m), out_shape=jax.ShapeDtypeS...]
where the time goes in v3:
time: 19.1 us; the launch traced here: 18.8 us
  Pallas kernels  16.1 us (84%)
  local copies, waits for them, and re-layouts  2.6 us (14%)
    pallas_call x1, Pallas kernels, body(): pl.pallas_call(functools.partial(kernel, n, m), out_shape=jax.ShapeDtypeS...  16.1 us
    unnamed x5, local copies, waits for them, and re-layouts  2.6 us

profile of v3, /device:TPU:1, one launch (start us, length us, event | category | flops | bytes accessed | tf_op | source)
XLA Modules:
  0.0 18.8 jit_solution(1075288963592763454)
XLA Ops:
  0.0 0.0 copy-start
  0.0 0.9 %copy-done = f32[4,64,256]{2,1,0:T(8,128)S(1)} copy-done((f32[4,64,256]{2,1,0:T(8,128)S(1)}, f32[4,64,256]{2,1,0:T(8,128)}, u32[]{:S(2)}) %copy-start) | copy-done | bytes 262168
  1.0 0.0 copy-start.1
  1.0 0.9 %copy-done.1 = s32[4,64,256]{2,1,0:T(8,128)S(1)} copy-done((s32[4,64,256]{2,1,0:T(8,128)S(1)}, s32[4,64,256]{2,1,0:T(8,128)}, u32[]{:S(2)}) %copy-start.1) | copy-done | bytes 262168
  1.9 16.1 %shard_map.28 = f32[4,64,256]{2,1,0:T(8,128)S(1)} custom-call(f32[4,64,256]{2,1,0:T(8,128)S(1)} %copy-done, s32[4,64,256]{2,1,0:T(8,128)S(1)} %copy-done.1), custom_call_target="tpu_custom_call" | custom-call | tf_op jit(solution)/shard_map/pallas_call | solution.py:453
  18.0 0.7 %copy.4 = f32[4,64,256]{2,1,0:T(8,128)} copy(f32[4,64,256]{2,1,0:T(8,128)S(1)} %shard_map.28) | data formatting | bytes 524288
Async XLA Ops:
  0.0 0.9 %copy-start = (f32[4,64,256]{2,1,0:T(8,128)S(1)}, f32[4,64,256]{2,1,0:T(8,128)}, u32[]{:S(2)}) copy-start(f32[4,64,256]{2,1,0:T(8,128)} %source_ref.1) | copy-start | bytes 786436
  1.0 0.9 %copy-start.1 = (s32[4,64,256]{2,1,0:T(8,128)S(1)}, s32[4,64,256]{2,1,0:T(8,128)}, u32[]{:S(2)}) copy-start(s32[4,64,256]{2,1,0:T(8,128)} %obstacle_ref.1) | copy-start | bytes 786436

commit v4 on v3

--- a/solution.py
+++ b/solution.py
@@ -452,7 +452,7 @@
         vmem = pl.BlockSpec(memory_space=pltpu.VMEM)
         return pl.pallas_call(
             functools.partial(kernel, n, m),
-            out_shape=jax.ShapeDtypeStruct(source.shape, F32),
+            out_shape=pltpu.VMEM(source.shape, F32),
             in_specs=[pl.BlockSpec(memory_space=pltpu.HBM)] * 2,
             out_specs=vmem,
             scratch_shapes=[
@@ -486,7 +486,7 @@
                 pltpu.SemaphoreType.REGULAR,
             ],
             compiler_params=pltpu.CompilerParams(
-                collective_id=0, has_side_effects=True, vmem_limit_bytes=32 * 1024 * 1024
+                collective_id=0, has_side_effects=True, vmem_limit_bytes=56 * 1024 * 1024
             ),
         )(source, obstacle)
 

time: 19.1 us -> 17.1 us (0.90)
  local copies, waits for them, and re-layouts: 2.6 us -> 0.71 us
    unnamed x5 -> x1, local copies, waits for them, and re-layouts: 2.6 us -> 0.71 us
where the time goes in v4:
time: 17.1 us; the launch traced here: 16.8 us
  Pallas kernels  16.1 us (94%)
  local copies, waits for them, and re-layouts  0.71 us (4%)
    pallas_call x1, Pallas kernels, body(): pl.pallas_call(functools.partial(kernel, n, m), out_shape=pltpu.VMEM(sour...  16.1 us
    unnamed x1, local copies, waits for them, and re-layouts  0.71 us

profile of v4, /device:TPU:1, one launch (start us, length us, event | category | flops | bytes accessed | tf_op | source)
XLA Modules:
  0.0 16.8 jit_solution(9720568125441732226)
XLA Ops:
  0.0 16.1 %shard_map.28 = f32[4,64,256]{2,1,0:T(8,128)S(1)} custom-call(f32[4,64,256]{2,1,0:T(8,128)} %source_ref.1, s32[4,64,256]{2,1,0:T(8,128)} %obstacle_ref.1), custom_call_target="tpu_custom_call" | custom-call | tf_op jit(solution)/shard_map/pallas_call | solution.py:453
  16.1 0.7 %copy.4 = f32[4,64,256]{2,1,0:T(8,128)} copy(f32[4,64,256]{2,1,0:T(8,128)S(1)} %shard_map.28) | data formatting | bytes 524288
